TPU v7x, 256 devices: a whole 4x4x8 slice. The times are simulated.
256 devices in a mesh: ctx: 16 (over z, core), ch: 16 (over x, y).
Axes of the slice: x: 4, y: 4, z: 8, core: 2. Of those that a mesh axis runs over, the one named last changes fastest.
Arguments:
- tokens: bfloat16 [24576, 4096], P('ctx', 'ch'), may hold values from -6 to 6
- in_weight: bfloat16 [4096, 3, 4096], P('ctx', None, 'ch'), may hold values from -0.09375 to 0.09375
- short_taps: float32 [3, 3, 4096], P(None, None, 'ch'), may hold values from -3 to 3
- residues: float32 [16, 4096], P(None, 'ch'), may hold values from -0.6 to 0.6
- decay_rates: float32 [16, 4096], P(None, 'ch'), may hold values from 2.0345053e-05 to 0.05
- skip_gain: float32 [4096], P('ch'), may hold values from -4 to 4
Outputs:
- mixed: bfloat16 [24576, 4096], P('ctx', 'ch')
All inputs are finite; a program needn't handle non-finite values.
Results may differ from a plain program's by a relative error of at most 0.0065.
Values may be sent and summed in bfloat16 or wider, within the bound.
A program may use at most 128 MiB of HBM per device.

v0:
```python
import jax
import jax.numpy as jnp
from jax import lax
from jax.sharding import PartitionSpec as P

BLOCK = 32


def shifted(block, axis, distance):
    devices = range(lax.axis_size(axis))
    route = [(i - distance, i) for i in devices if i - distance in devices]
    return lax.ppermute(block, axis, route)


def entering_2(value, axis, combine, identity):
    size, index = (lax.axis_size(axis), lax.axis_index(axis))
    everything = jax.tree.map(lambda part: lax.all_gather(part, axis), value)
    start = jax.tree.map(
        lambda part, zero: jnp.broadcast_to(jnp.asarray(zero, part.dtype), part.shape),
        value,
        identity,
    )

    def step(k, before):
        reached = k < index
        new = combine(before, jax.tree.map(lambda part: part[k], everything))
        return jax.tree.map(lambda a, b: jnp.where(reached, a, b), new, before)

    return lax.fori_loop(0, size, step, start)


def combine_pairs(earlier, later):
    return (earlier[0] * later[0], later[0] * earlier[1] + later[1])


def body(tokens, in_weight, short_taps, residues, decay_rates, skip_gain):
    rows = tokens.shape[0]
    chans = in_weight.shape[2]
    poles = residues.shape[0]
    taps = short_taps.shape[1]
    whole = lax.all_gather(tokens, "ch", axis=1, tiled=True)
    piece = lax.all_gather(in_weight, "ctx", axis=0, tiled=True)
    width = piece.shape[0]
    summed = jnp.dot(whole, piece.reshape(width, 3 * chans), preferred_element_type=jnp.float32)
    projected = summed.reshape(rows, 3, chans).astype(jnp.bfloat16)
    before = shifted(projected[rows - (taps - 1) :], "ctx", 1)
    extended = jnp.concatenate([before, projected], axis=0).astype(jnp.float32)
    featured = jnp.zeros((rows, 3, chans), jnp.float32)
    for shift in range(taps):
        featured = (
            featured
            + short_taps[:, shift, :] * extended[taps - 1 - shift : taps - 1 - shift + rows]
        )
    query = featured[:, 0]
    gated = (featured[:, 1] * featured[:, 2]).astype(jnp.bfloat16)
    values = gated.astype(jnp.float32)
    nblocks = rows // BLOCK
    blocks = values.reshape(nblocks, BLOCK, chans)
    lags = jnp.arange(BLOCK, dtype=jnp.float32)
    offsets = lags[:, None] - lags[None, :]
    causal = offsets >= 0
    spans = jnp.maximum(offsets, 0.0)[:, :, None]
    toeplitz = jnp.zeros((BLOCK, BLOCK, chans), jnp.float32)
    for mode in range(poles):
        toeplitz = toeplitz + residues[mode] * jnp.exp(-decay_rates[mode] * spans)
    toeplitz = jnp.where(causal[:, :, None], toeplitz, 0.0)
    inner = jnp.einsum("ijc,bjc->bic", toeplitz, blocks, precision=lax.Precision.HIGHEST)
    tails = jnp.exp(-decay_rates[None] * (BLOCK - 1 - lags)[:, None, None])
    ends = jnp.einsum("jnc,bjc->bnc", tails, blocks, precision=lax.Precision.HIGHEST)
    step_decay = jnp.broadcast_to(jnp.exp(-decay_rates * BLOCK)[None], ends.shape)
    running = lax.associative_scan(combine_pairs, (step_decay, ends), axis=0)[1]
    local_in = jnp.concatenate([jnp.zeros((1, poles, chans), jnp.float32), running[:-1]], axis=0)
    device_decay = jnp.exp(-decay_rates * rows)
    identity = (jnp.ones((poles, chans), jnp.float32), jnp.zeros((poles, chans), jnp.float32))
    incoming = entering_2((device_decay, running[-1]), "ctx", combine_pairs, identity)[1]
    block_starts = (BLOCK * jnp.arange(nblocks, dtype=jnp.float32))[:, None, None]
    entering = local_in + jnp.exp(-decay_rates[None] * block_starts) * incoming[None]
    leads = residues[None] * jnp.exp(-decay_rates[None] * (lags + 1.0)[:, None, None])
    across = jnp.einsum("inc,bnc->bic", leads, entering, precision=lax.Precision.HIGHEST)
    conv = (inner + across).reshape(rows, chans)
    return (query * (conv + skip_gain * values)).astype(jnp.bfloat16)


def solution(mesh):
    in_specs = (
        P("ctx", "ch"),
        P("ctx", None, "ch"),
        P(None, None, "ch"),
        P(None, "ch"),
        P(None, "ch"),
        P("ch"),
    )
    out_specs = P("ctx", "ch")
    return jax.shard_map(body, mesh=mesh, in_specs=in_specs, out_specs=out_specs, check_vma=False)
```

profile of v0, /device:TPU:1, one launch (start us, length us, event | category | flops | bytes accessed | tf_op | source)
XLA Modules:
  0.0 322.2 jit_solution(10529097800440755126)
XLA Ops:
  6.5 1.9 copy.97
  10.3 1.3 multiply_exponential_fusion
  11.7 23.7 %all-gather = f32[256,256]{1,0:T(8,128)} all-gather(f32[16,256]{1,0:T(8,128)S(1)} %get-tuple-element.141), channel_id=2, replica_groups=mesh['ctx'=16,'ch'=16] {'ctx'}, dimensions={0}, use_global_device_ids=true | all-gather | bytes 278528 | tf_op jit(solution)/shard_map/all_gather | solution.py:17
  35.4 2.9 add_select_fusion
  38.4 31.8 %all-gather.6.cloned.1.call-done = bf16[4096,3,256]{0,2,1:T(8,128)(2,1)} async-done(((bf16[256,3,256]{0,2,1:T(8,128)(2,1)}), bf16[4096,3,256]{0,2,1:T(8,128)(2,1)}) %all-gather.6.cloned.1.call-update) | async-done | bytes 6291472 | tf_op jit(solution)/shard_map/all_gather | solution.py:42
  70.2 105.8 %all-gather.4.cloned.1.call-done = bf16[1536,4096]{1,0:T(8,128)(2,1)} async-done(((bf16[1536,256]{1,0:T(8,128)(2,1)}), bf16[1536,4096]{1,0:T(8,128)(2,1)}) %all-gather.4.cloned.1.call-update) | async-done | bytes 12582928 | tf_op jit(solution)/shard_map/all_gather | solution.py:41
  176.0 14.8 %fusion.6 = bf16[1536,3,256]{2,0,1:T(8,128)(2,1)S(1)} fusion(bf16[4096,3,256]{0,2,1:T(8,128)(2,1)} %all-gather.6.cloned.1.call-done, bf16[1536,4096]{1,0:T(8,128)(2,1)} %all-gather.4.cloned.1.call-done), kind=kOutput, calls=%fused_computation.12 | convolution fusion | flops 9664856064 | bytes 21233664 | tf_op jit(solution)/shard_map/dot_general | solution.py:44
  190.8 4.8 %collective-permute-start = (bf16[2,3,256]{2,0,1:T(2,128)(2,1)S(1)}, bf16[2,3,256]{2,0,1:T(2,128)(2,1)S(1)}, u32[]{:S(2)}, u32[]{:S(2)}) collective-permute-start(bf16[2,3,256]{2,0,1:T(2,128)(2,1)S(1)} %slice.313), channel_id=1, source_target_pairs={{0,16},{16,32},{32,48},{48,64},{64,80},{80,96},{96,112},{112,128},... | collective-permute-start | bytes 9224 | tf_op jit(solution)/shard_map/ppermute | solution.py:12
  196.1 0.7 copy.103
  196.9 4.5 %copy.99 = f32[32,32,256]{1,0,2:T(8,128)} copy(f32[32,32,256]{2,1,0:T(8,128)S(1)} %add_select_fusion) | data formatting | bytes 2097152 | tf_op jit(solution)/shard_map/jit(_where)/select_n | solution.py:66
  201.9 1.4 fusion.4
  203.3 2.1 copy-done
  205.6 3.3 %copy.98 = bf16[48,32,256]{0,1,2:T(8,128)(2,1)S(1)} copy(bf16[48,32,256]{2,1,0:T(8,128)(2,1)S(1)} %bitcast.96) | data formatting | bytes 1572864 | tf_op jit(solution)/shard_map/convert_element_type | solution.py:55
  209.0 3.3 %fusion.14 = f32[256,48,16]{1,2,0:T(8,128)} fusion(bf16[48,32,256]{0,1,2:T(8,128)(2,1)S(1)} %copy.98, f32[32]{0:T(128)S(1)} %copy-done.16, f32[16,256]{0,1:T(8,128)S(1)} %copy.100), kind=kOutput, calls=%fused_computation.17 | convolution fusion | flops 75628544 | bytes 1589376 | tf_op jit(solution)/shard_map/jnc,bjc->bnc/dot_general | solution.py:69
  212.2 2.8 copy.102
  215.1 0.7 slice_add_fusion.3
  217.8 0.7 pad.32
  218.5 0.8 fusion.31
  219.3 1.3 pad_add_fusion
  221.4 1.9 pad.34
  223.2 2.7 pad.35
  225.9 1.6 add.194
  227.5 1.6 fusion.28
  229.1 2.2 pad.37
  231.3 1.5 pad_maximum_fusion.2
  232.8 4.1 %pad.36 = f32[12,16,256]{2,1,0:T(8,128)} pad(f32[6,16,256]{2,1,0:T(8,128)} %pad_maximum_fusion.2, f32[]{:T(128)} %constant.35.clone.1), padding=0_1_1x0_0_0x0_0_0 | pad | bytes 294916 | tf_op jit(solution)/shard_map/pad | solution.py:71
  236.9 1.0 fusion.27
  237.8 1.0 add.196
  238.8 4.4 %pad.38 = f32[24,16,256]{2,1,0:T(8,128)} pad(f32[12,16,256]{2,1,0:T(8,128)S(1)} %pad_maximum_fusion.1, f32[]{:T(128)} %constant.35.clone.1), padding=0_1_1x0_0_0x0_0_0 | pad | bytes 589828 | tf_op jit(solution)/shard_map/pad | solution.py:71
  243.2 4.4 %pad.39 = f32[24,16,256]{2,1,0:T(8,128)} pad(f32[12,16,256]{2,1,0:T(8,128)S(1)} %add.196, f32[]{:T(128)} %constant.35.clone.1), padding=1_0_1x0_0_0x0_0_0 | pad | bytes 589828 | tf_op jit(solution)/shard_map/pad | solution.py:71
  247.6 1.2 add.198
  248.8 1.9 fusion.26
  250.9 8.1 %pad.77 = f32[47,16,256]{2,1,0:T(8,128)} pad(f32[24,16,256]{2,1,0:T(8,128)S(1)} %add.198, f32[]{:T(128)} %constant.35.clone.1), padding=0_0_1x0_0_0x0_0_0 | pad | bytes 1163268
  259.1 6.4 %fusion.38 = f32[256,48,32]{1,2,0:T(8,128)} fusion(bf16[48,32,256]{0,1,2:T(8,128)(2,1)S(1)} %copy.98, f32[32,32,256]{1,0,2:T(8,128)} %copy.99), kind=kOutput, calls=%fused_computation.91 | convolution fusion | flops 150994944 | bytes 3407872 | tf_op jit(solution)/shard_map/ijc,bjc->bic/dot_general | solution.py:67
  265.8 17.1 %all_gather.19 = f32[16,16,256]{2,1,0:T(8,128)S(1)} all-gather(f32[1,16,256]{2,1,0:T(8,128)S(1)} %slice-done), channel_id=1, replica_groups=mesh['ctx'=16,'ch'=16] {'ctx'}, dimensions={0}, use_global_device_ids=true | all-gather | bytes 278528 | tf_op jit(solution)/shard_map/all_gather | solution.py:17
  282.8 11.6 %while.14 = (s32[]{:T(128)}, f32[16,256]{1,0:T(8,128)S(1)}, s32[]{:T(128)}, f32[16,16,256]{2,1,0:T(8,128)}, f32[16,16,256]{2,1,0:T(8,128)S(1)}, /*index=5*/s32[]{:T(128)}, s32[]{:T(128)}) while((s32[]{:T(128)}, f32[16,256]{1,0:T(8,128)S(1)}, s32[]{:T(128)}, f32[16,16,256]{2,1,0:T(8,128)}, f32[16,16,256]{2,1,0:T(8,128)S(1)}, ...), condition=%wide.region_1.2_spmd.clone, body=%wide.region_0.1_spmd.clone.sunk | while | flops 16388 | bytes 65645 | solution.py:29
  282.8 0.7 fusion.44
  283.5 0.7 fusion.44
  284.3 0.7 fusion.44
  285.0 0.7 fusion.44
  285.7 0.7 fusion.44
  286.4 0.7 fusion.44
  287.2 0.7 fusion.44
  287.9 0.7 fusion.44
  294.8 1.5 copy.104
  296.3 11.1 %add_bitcast_fusion = f32[48,32,256]{0,1,2:T(8,128)} fusion(f32[256,48,32]{1,2,0:T(8,128)} %fusion.38, f32[48,16,256]{0,1,2:T(8,128)S(1)} %copy.104, f32[32]{0:T(128)S(1)} %copy-done.15, f32[16,256]{0,1:T(8,128)S(1)} %copy-done.5, f32[16,256]{0,1:T(8,128)S(1)} %copy-done.3), kind=kOutput, calls=%fused_computation.11 | convolution fusion | flops 76152832 | bytes 3965056 | tf_op jit(solution)/shard_map/inc,bnc->bic/dot_general | solution.py:79
  307.4 4.3 %copy.105 = f32[48,32,256]{2,1,0:T(8,128)S(1)} copy(f32[48,32,256]{0,1,2:T(8,128)} %add_bitcast_fusion) | data formatting | bytes 3145728 | tf_op jit(solution)/shard_map/add | solution.py:80
  311.7 3.6 %fusion.19 = bf16[1536,256]{1,0:T(8,128)(2,1)} fusion(f32[1536,3,256]{2,0,1:T(8,128)} %copy-done, f32[48,32,256]{2,1,0:T(8,128)S(1)} %copy.105, f32[256]{0:T(256)S(1)} %copy-done.13), kind=kLoop, calls=%fused_computation.24 | loop fusion | flops 2752512 | bytes 7078912 | tf_op jit(solution)/shard_map/convert_element_type | solution.py:81
  (79 shorter events, 12.5 us)
Async XLA Ops:
  6.5 28.8 %copy-start.9 = (f32[16,256]{1,0:T(8,128)S(1)}, f32[16,256]{1,0:T(8,128)}, u32[]{:S(2)}) copy-start(f32[16,256]{1,0:T(8,128)} %param.12) | copy-start | bytes 49156
  6.5 28.8 %copy-start.12 = (f32[3,3,256]{2,1,0:T(4,128)S(1)}, f32[3,3,256]{2,1,0:T(4,128)}, u32[]{:S(2)}) copy-start(f32[3,3,256]{2,1,0:T(4,128)} %param.10) | copy-start | bytes 27652
  6.5 28.9 %copy-start.11 = (f32[16,256]{1,0:T(8,128)S(1)}, f32[16,256]{1,0:T(8,128)}, u32[]{:S(2)}) copy-start(f32[16,256]{1,0:T(8,128)} %param.11) | copy-start | bytes 49156
  6.5 63.7 %all-gather.6.cloned.1.call-start = ((), (), s32[]{:S(2)}) async-start(), calls=%async_computation.1 | async-start | bytes 6684672 | tf_op jit(solution)/shard_map/all_gather | solution.py:42
  8.5 167.5 %all-gather.4.cloned.1.call-start = ((), (), s32[]{:S(2)}) async-start(), calls=%async_computation | async-start | bytes 13369344 | tf_op jit(solution)/shard_map/all_gather | solution.py:41
  11.7 189.7 %copy-start.6 = (f32[16,256]{1,0:T(8,128)}, f32[16,256]{1,0:T(8,128)S(1)}, u32[]{:S(2)}) copy-start(f32[16,256]{1,0:T(8,128)S(1)} %get-tuple-element.146) | copy-start | bytes 49156
  11.7 203.4 %copy-start.8 = (f32[16,256]{1,0:T(8,128)}, f32[16,256]{1,0:T(8,128)S(1)}, u32[]{:S(2)}) copy-start(f32[16,256]{1,0:T(8,128)S(1)} %get-tuple-element.145) | copy-start | bytes 49156
  190.8 10.7 %collective-permute-start = (bf16[2,3,256]{2,0,1:T(2,128)(2,1)S(1)}, bf16[2,3,256]{2,0,1:T(2,128)(2,1)S(1)}, u32[]{:S(2)}, u32[]{:S(2)}) collective-permute-start(bf16[2,3,256]{2,0,1:T(2,128)(2,1)S(1)} %slice.313), channel_id=1, source_target_pairs={{0,16},{16,32},{32,48},{48,64},{64,80},{80,96},{96,112},{112,128},... | collective-permute-start | bytes 9224 | tf_op jit(solution)/shard_map/ppermute | solution.py:12
  201.4 7.5 %copy-start.2 = (f32[16,256]{0,1:T(8,128)}, f32[16,256]{0,1:T(8,128)S(1)}, u32[]{:S(2)}) copy-start(f32[16,256]{0,1:T(8,128)S(1)} %copy.100) | copy-start | bytes 49156
  203.3 2.2 copy-start
  205.6 3.3 %copy-start.16 = (f32[32]{0:T(128)S(1)}, f32[32]{0:T(128)}, u32[]{:S(2)}) copy-start(f32[32]{0:T(128)} %iota_subtract_fusion.1) | copy-start | bytes 388
  212.2 4.3 %copy-start.10 = (f32[16,256]{1,0:T(8,128)S(1)}, f32[16,256]{1,0:T(8,128)}, u32[]{:S(2)}) copy-start(f32[16,256]{1,0:T(8,128)} %get-tuple-element.142) | copy-start | bytes 49156
  215.9 0.6 copy-start.4
  259.1 6.4 %copy-start.1 = (f32[23,16,256]{2,1,0:T(8,128)S(1)}, f32[23,16,256]{2,1,0:T(8,128)}, u32[]{:S(2)}) copy-start(f32[23,16,256]{2,1,0:T(8,128)} %fusion.26) | copy-start | bytes 1130500
  259.1 6.7 %slice-start = ((f32[47,16,256]{2,1,0:T(8,128)}), f32[1,16,256]{2,1,0:T(8,128)S(1)}, s32[]{:S(2)}) async-start(f32[47,16,256]{2,1,0:T(8,128)} %pad.77), calls=%async_computation.2 | async-start | bytes 32768 | tf_op jit(solution)/shard_map/slice | solution.py:75
  265.5 29.1 %copy-start.7 = (f32[16,256]{1,0:T(8,128)S(1)}, f32[16,256]{1,0:T(8,128)}, u32[]{:S(2)}) copy-start(f32[16,256]{1,0:T(8,128)} %copy-done.6) | copy-start | bytes 49156
  265.5 29.1 %copy-start.14 = (f32[48]{0:T(128)S(1)}, f32[48]{0:T(128)}, u32[]{:S(2)}) copy-start(f32[48]{0:T(128)} %iota_multiply_fusion) | copy-start | bytes 580
  294.5 1.8 copy-start.3
  294.5 1.8 copy-start.5
  294.6 1.8 copy-start.15
  307.4 4.3 %copy-start.13 = (f32[256]{0:T(256)S(1)}, f32[256]{0:T(256)}, u32[]{:S(2)}) copy-start(f32[256]{0:T(256)} %param.13) | copy-start | bytes 3076
Sparse Core Ops, SparseCore 0:
  9.1 61.0 all-gather.5
  72.6 103.3 all-gather.3
where the time goes:
time: 325 us; the launch traced here: 322 us
  waiting for transfers between devices  138 us (42%)
  local copies, waits for them, and re-layouts  50.9 us (16%)
  blocking collectives  40.7 us (13%)
  other arithmetic  38.1 us (12%)
  matrix products  35.5 us (11%)
  between operations  13.8 us (4%)
  starting transfers between devices  4.83 us (1%)
    all_gather x1, waiting for transfers between devices, body(): whole = lax.all_gather(tokens, 'ch', axis=1, tiled=True)  106 us
    all_gather x2, blocking collectives, entering_2(): everything = jax.tree.map(lambda part: lax.all_gather(part, axis), value)  40.7 us
    all_gather x1, waiting for transfers between devices, body(): piece = lax.all_gather(in_weight, 'ctx', axis=0, tiled=True)  31.8 us
    pad x9, local copies, waits for them, and re-layouts, body(): running = lax.associative_scan(combine_pairs, (step_decay, ends), axis=0)[1]  20.7 us
    dot_general x1, matrix products, body(): jnp.dot(whole, piece.reshape(width, 3 * chans), preferred_element_type=jn...  14.8 us
    unnamed x39, local copies, waits for them, and re-layouts  13 us
    select_n x16, other arithmetic, step(): return jax.tree.map(lambda a, b: jnp.where(reached, a, b), new, before)  11.6 us
    dot_general x1, matrix products, body(): jnp.einsum('inc,bnc->bic', leads, entering, precision=lax.Precision.HIGHEST)  11.1 us
  transfers between devices with their start and end apart: 3, of which 2 were waited for; matrix products, arithmetic and copies ran while one was open for 3% of the time, Pallas kernels for 0%

commit v1 on v0

v1 whole, which is shorter than its diff:
```python
import functools

import jax
import jax.numpy as jnp
from jax import lax
from jax.experimental import pallas as pl
from jax.experimental.pallas import tpu as pltpu
from jax.sharding import PartitionSpec as P

MESH = pl.DeviceIdType.MESH
F32 = jnp.float32
BF16 = jnp.bfloat16
L = 16
GROUP = 8 * L
HALO = 8
CHUNKS = ((1408, 128), (0, 256), (256, 256), (512, 256), (768, 256), (1024, 256), (1280, 128))


def kernel(
    tokens, weight, taps, residues, decay, skip, out,
    tok, w, proj, query, base, states, mixed, carry, lam, filt, scan, bdec, gdec, lead, tapb, skipb,
    final, landed, entry,
    s_send, s_recv, w_send_sem, w_recv_sem, h_send, h_recv, f_send, f_recv, local,
):
    ch, ctx = lax.axis_index("ch"), lax.axis_index("ctx")
    x, y, z, core = ch // 4, ch % 4, ctx // 2, ctx % 2
    sibling = z * 2 + 1 - core
    rows = tokens.shape[0]
    poles = residues.shape[0]
    groups = rows // GROUP
    nctx = 16

    def near(axis, d):
        return {"ch": (x + d) % 4 * 4 + y if axis == "x" else x * 4 + (y + d) % 4}

    own_tok = pltpu.make_async_copy(tokens, tok.at[x, y], local.at[0])
    own_w = pltpu.make_async_copy(weight, w.at[pl.ds(ctx * 256, 256)], local.at[1])
    own_tok.start()
    own_w.start()
    barrier = pltpu.get_barrier_semaphore()
    for axis in "xy":
        for d in (1, 3):
            pl.semaphore_signal(barrier, 1, device_id=near(axis, d), device_id_type=MESH)
    for o in range(1, nctx):
        pl.semaphore_signal(barrier, 1, device_id={"ctx": (ctx + o) % nctx}, device_id_type=MESH)
    pl.semaphore_wait(barrier, 4 + nctx - 1)
    own_tok.wait()
    own_w.wait()

    sent = []
    copies = {}

    def send(key, ref, to, ss, rs):
        copy = pltpu.make_async_remote_copy(
            src_ref=ref, dst_ref=ref, send_sem=ss, recv_sem=rs, device_id=to, device_id_type=MESH
        )
        copy.start()
        sent.append(copy)
        copies[key] = copy

    def halves(r):
        first, size = CHUNKS[r]
        return (("x", "y", first, size // 2, 0), ("y", "x", first + size // 2, size // 2, 1))

    def stage(r, number, forward):
        for one, two, first, size, h in halves(r):
            axis = one if number == 1 else two
            for i, d in enumerate((1, 3)):
                k = (number - 1) * 8 + forward * 4 + h * 2 + i
                at_x, at_y, start, count = x, y, first, size
                if forward:
                    copies[r, number, 0, h, i].wait_recv()
                    if axis == "x":
                        at_x = (x - d) % 4
                    else:
                        at_y = (y - d) % 4
                    start, count = first + i * (size // 2), size // 2
                span = pl.ds(start, count)
                if number == 1:
                    ref = tok.at[at_x, at_y, span]
                elif axis == "x":
                    ref = tok.at[at_x, :, span]
                else:
                    ref = tok.at[:, at_y, span]
                send((r, number, forward, h, i), ref, near(axis, d), s_send.at[r, k], s_recv.at[r, k])

    def landed_stage(r, number):
        for h in (0, 1):
            for i in (0, 1):
                copies[r, number, 1, h, i].wait_recv()

    def weights(s):
        for i, d in enumerate((1, 7)):
            owner = (z - d * s) % 8 * 2 + core
            for part in (0, 1):
                if s > 0:
                    if s == 4 and part != i:
                        continue
                    copies["w", s - 1, i, part].wait_recv()
                ref = w.at[pl.ds(owner * 256 + part * 128, 128)]
                if s < 3 or (s == 3 and part == i):
                    to = {"ctx": (z + d) % 8 * 2 + core}
                    send(("w", s, i, part), ref, to, w_send_sem.at[s, i, part], w_recv_sem.at[s, i, part])
                if s > 0 or i == 0:
                    send(
                        ("s", s, i, part), ref, {"ctx": sibling},
                        w_send_sem.at[s, 2 + i, part], w_recv_sem.at[s, 2 + i, part],
                    )

    def tables():
        ids = lax.broadcasted_iota(jnp.int32, (8, 128), 0)
        lanes8 = ids.astype(F32)
        for t in (0, 1):
            cols = pl.ds(t * 128, 128)
            for g in range(3):
                for k in range(3):
                    tapb[t, g * 3 + k] = jnp.broadcast_to(taps[g, k : k + 1, cols], (8, 128))
            skipb[t] = jnp.broadcast_to(skip[:, cols], (8, 128))
            for m in range(L):
                filt[t, m] = jnp.zeros((8, 128), F32)
            for n in range(poles):
                lam[t, n] = jnp.broadcast_to(decay[n : n + 1, cols], (8, 128))
                lead[t, n] = jnp.broadcast_to(residues[n : n + 1, cols], (8, 128))

            def mode(n, _):
                rate, gain = lam[t, n], lead[t, n]
                step = jnp.exp(-rate)
                lam[t, n] = step
                lead[t, n] = gain * step
                for k, s in enumerate((1, 2, 4)):
                    scan[t, k, n] = jnp.where(ids >= s, jnp.exp(-rate * float(L * s)), 0.0)
                bdec[t, n] = jnp.exp(-rate * (lanes8 * float(L)))
                gdec[t, n] = jnp.exp(-rate * float(GROUP))
                carry[t, n] = jnp.zeros((8, 128), F32)
                for m in range(L):
                    filt[t, m] += gain * jnp.exp(-rate * float(m))
                return 0

            lax.fori_loop(0, poles, mode, 0)

    def project(first, size):
        span = pl.ds(first, size)
        left = jnp.concatenate([tok[i // 4, i % 4, span, :] for i in range(16)], axis=1)
        for g in range(3):
            total = jnp.dot(left, w[:, g * 256 : (g + 1) * 256], preferred_element_type=F32)
            total = total.astype(BF16).astype(F32)
            for t in (0, 1):
                proj[g * 2 + t, pl.ds(HALO + first, size), :] = total[:, t * 128 : (t + 1) * 128]

    def filter_group(g, t):
        first = HALO + g * GROUP
        ids = lax.broadcasted_iota(jnp.int32, (8, 128), 0)

        def rows_at(part, i):
            return proj[part * 2 + t, pl.ds(first + i, 8, stride=L), :]

        feats = []
        for part in range(3):
            k0, k1, k2 = (tapb[t, part * 3 + k] for k in range(3))
            two, one = rows_at(part, -2), rows_at(part, -1)
            listed = []
            for i in range(L):
                now = rows_at(part, i)
                value = k0 * now + k1 * one + k2 * two
                if part == 0:
                    query[g, t, i] = value
                else:
                    listed.append(value)
                two, one = one, now
            feats.append(listed)
        gated = [(a * b).astype(BF16).astype(F32) for a, b in zip(feats[1], feats[2])]

        for n in range(poles):
            step = lam[t, n]
            end = gated[0]
            for i in range(1, L):
                end = step * end + gated[i]
            for k, s in enumerate((1, 2, 4)):
                end = end + scan[t, k, n] * pltpu.roll(end, s, axis=0)
            before = jnp.where(ids >= 1, pltpu.roll(end, 1, axis=0), 0.0)
            held = carry[t, n]
            states[g, t, n] = before + bdec[t, n] * held
            carry[t, n] = jnp.broadcast_to(end[7:8], (8, 128)) + gdec[t, n] * held

        for i in range(L):
            total = skipb[t] * gated[i]
            for j in range(i + 1):
                total = total + filt[t, i - j] * gated[j]
            base[g, t, i] = total

    def filter_groups(lo, hi):
        def step(k, _):
            filter_group(lo + k // 2, k % 2)
            return 0

        lax.fori_loop(0, 2 * (hi - lo), step, 0)

    def finish(k, _):
        g, t = k // 2, k % 2
        flow = []
        for n in range(poles):
            held = entry[t, n]
            flow.append(lead[t, n] * (states[g, t, n] + bdec[t, n] * held))
            entry[t, n] = gdec[t, n] * held
        steps = [lam[t, n] for n in range(poles)]
        for i in range(L):
            parts = flow
            while len(parts) > 1:
                parts = [a + b for a, b in zip(parts[::2], parts[1::2])]
            mixed[t, pl.ds(g * GROUP + i, 8, stride=L), :] = query[g, t, i] * (base[g, t, i] + parts[0])
            if i < L - 1:
                flow = [a * b for a, b in zip(flow, steps)]
        span = pl.ds(pl.multiple_of(g * GROUP, GROUP), GROUP)
        out[span, pl.ds(pl.multiple_of(t * 128, 128), 128)] = mixed[t, span, :].astype(BF16)
        return 0

    count = len(CHUNKS)
    weights(0)
    for r in range(count):
        stage(r, 1, 0)
    tables()
    for r in range(count):
        stage(r, 1, 1)
    weights(1)
    landed_stage(0, 1)
    stage(0, 2, 0)
    landed_stage(1, 1)
    stage(1, 2, 0)
    for r in range(2, count):
        landed_stage(r, 1)

    def tick(r):
        stage(r, 2, 1)
        if r + 2 < count:
            stage(r + 2, 2, 0)

    def compute(r):
        landed_stage(r, 2)
        first, size = CHUNKS[r]
        if size == 128:
            project(first, size)
        else:
            for half in range(0, size, 256):
                project(first + half, 256)

    tick(0)
    weights(2)
    tick(1)
    weights(3)
    tick(2)
    weights(4)
    for key, copy in copies.items():
        if key[0] == "s":
            copy.wait_recv()
    compute(0)
    halo = pltpu.make_async_remote_copy(
        src_ref=proj.at[:, pl.ds(rows, HALO)], dst_ref=proj.at[:, pl.ds(0, HALO)],
        send_sem=h_send, recv_sem=h_recv,
        device_id={"ctx": (ctx + 1) % nctx}, device_id_type=MESH,
    )

    @pl.when(ctx == 0)
    def _():
        proj[:, pl.ds(0, HALO), :] = jnp.zeros((6, HALO, 128), F32)

    @pl.when(ctx < nctx - 1)
    def _():
        halo.start()

    compute(1)

    @pl.when(ctx > 0)
    def _():
        halo.wait_recv()

    filter_groups(0, 2)
    tick(3)
    compute(2)
    filter_groups(2, 4)
    tick(4)
    compute(3)
    filter_groups(4, 6)
    tick(5)
    compute(4)
    filter_groups(6, 8)
    tick(6)
    compute(5)
    filter_groups(8, 10)
    compute(6)
    filter_groups(10, 12)

    for t in (0, 1):
        for n in range(poles):
            final[n : n + 1, t * 128 : (t + 1) * 128] = carry[t, n, 0:1, :]

    def exchange(o):
        return pltpu.make_async_remote_copy(
            src_ref=final, dst_ref=landed.at[ctx],
            send_sem=f_send.at[o], recv_sem=f_recv.at[o],
            device_id={"ctx": (ctx + o) % nctx}, device_id_type=MESH,
        )

    for o in range(1, nctx):

        @pl.when(ctx + o < nctx)
        def _():
            exchange(o).start()

    for o in range(1, nctx):

        @pl.when(ctx >= o)
        def _():
            pltpu.make_async_remote_copy(
                src_ref=final, dst_ref=landed.at[(ctx - o) % nctx],
                send_sem=f_send.at[o], recv_sem=f_recv.at[o],
                device_id={"ctx": (ctx + o) % nctx}, device_id_type=MESH,
            ).wait_recv()

    across = jnp.exp(-decay[...] * float(rows))

    def join(k, total):
        return across * total + landed[k]

    incoming = lax.fori_loop(0, ctx, join, jnp.zeros((poles, 256), F32))
    for t in (0, 1):
        for n in range(poles):
            entry[t, n] = jnp.broadcast_to(incoming[n : n + 1, t * 128 : (t + 1) * 128], (8, 128))
    lax.fori_loop(0, 2 * groups, finish, 0)

    for copy in sent:
        copy.wait_send()

    @pl.when(ctx < nctx - 1)
    def _():
        halo.wait_send()

    for o in range(1, nctx):

        @pl.when(ctx + o < nctx)
        def _():
            exchange(o).wait_send()


def body(tokens, in_weight, short_taps, residues, decay_rates, skip_gain):
    rows, poles = tokens.shape[0], residues.shape[0]
    groups = rows // GROUP
    flops = 2 * rows * 4096 * 768
    dma = pltpu.SemaphoreType.DMA
    vmem, anywhere = pl.BlockSpec(memory_space=pltpu.VMEM), pl.BlockSpec(memory_space=pl.ANY)
    return pl.pallas_call(
        kernel,
        out_shape=jax.ShapeDtypeStruct((rows, 256), BF16),
        in_specs=[anywhere, anywhere, vmem, vmem, vmem, vmem],
        out_specs=vmem,
        scratch_shapes=[
            pltpu.VMEM((4, 4, rows, 256), BF16),
            pltpu.VMEM((4096, 768), BF16),
            pltpu.VMEM((6, HALO + rows, 128), F32),
            pltpu.VMEM((groups, 2, L, 8, 128), F32),
            pltpu.VMEM((groups, 2, L, 8, 128), F32),
            pltpu.VMEM((groups, 2, poles, 8, 128), F32),
            pltpu.VMEM((2, rows, 128), F32),
            pltpu.VMEM((2, poles, 8, 128), F32),
            pltpu.VMEM((2, poles, 8, 128), F32),
            pltpu.VMEM((2, L, 8, 128), F32),
            pltpu.VMEM((2, 3, poles, 8, 128), F32),
            pltpu.VMEM((2, poles, 8, 128), F32),
            pltpu.VMEM((2, poles, 8, 128), F32),
            pltpu.VMEM((2, poles, 8, 128), F32),
            pltpu.VMEM((2, 9, 8, 128), F32),
            pltpu.VMEM((2, 8, 128), F32),
            pltpu.VMEM((poles, 256), F32),
            pltpu.VMEM((16, poles, 256), F32),
            pltpu.VMEM((2, poles, 8, 128), F32),
            dma((len(CHUNKS), 16)),
            dma((len(CHUNKS), 16)),
            dma((5, 4, 2)),
            dma((5, 4, 2)),
            dma(()),
            dma(()),
            dma((16,)),
            dma((16,)),
            dma((2,)),
        ],
        compiler_params=pltpu.CompilerParams(
            collective_id=0, has_side_effects=True, vmem_limit_bytes=56 * 2**20
        ),
        cost_estimate=pl.CostEstimate(flops=flops, bytes_accessed=4 * 2**20, transcendentals=0),
    )(tokens, in_weight.reshape(256, 768), short_taps, residues, decay_rates, skip_gain.reshape(1, 256))


def solution(mesh):
    in_specs = (
        P("ctx", "ch"),
        P("ctx", None, "ch"),
        P(None, None, "ch"),
        P(None, "ch"),
        P(None, "ch"),
        P("ch"),
    )
    return jax.shard_map(body, mesh=mesh, in_specs=in_specs, out_specs=P("ctx", "ch"), check_vma=False)
```

time: 325 us -> 95.1 us (0.29)
  the two profiles are of different devices: /device:TPU:1 before, /device:TPU:199 now
where the time goes in v1:
time: 95.1 us; the launch traced here: 94.9 us
  Pallas kernels  90.8 us (95%)
  local copies, waits for them, and re-layouts  4.15 us (4%)
    pallas_call x1, Pallas kernels, body(): pl.pallas_call(kernel, out_shape=jax.ShapeDtypeStruct((rows, 256), BF16),...  90.8 us
    unnamed x2, local copies, waits for them, and re-layouts  3.23 us

profile of v1, /device:TPU:199, one launch (start us, length us, event | category | flops | bytes accessed | tf_op | source)
XLA Modules:
  0.0 94.9 jit_solution(17118621169284786382)
XLA Ops:
  0.0 1.2 %copy.8 = bf16[256,3,256]{0,2,1:T(8,128)(2,1)S(1)} copy(bf16[256,3,256]{2,0,1:T(8,128)(2,1)} %param.7) | data formatting | bytes 786432 | tf_op args[1]
  1.2 0.9 copy.9.weight
  2.1 90.8 %shard_map.64 = bf16[1536,256]{1,0:T(8,128)(2,1)} custom-call(bf16[1536,256]{1,0:T(8,128)(2,1)} %tokens.1, bf16[256,768]{1,0:T(8,128)(2,1)} %copy.9.weight, f32[3,3,256]{2,1,0:T(4,128)} %taps.1, f32[16,256]{1,0:T(8,128)} %residues.1, f32[16,256]{1,0:T(8,128)} %decay.1, f32[1,256]{1,0:T(1,128)} %bitcast.3), custom_call_target="tpu_custom_call" | custom-call | flops 9663676416 | bytes 4194304 | tf_op jit(solution)/shard_map/pallas_call | solution.py:350
  92.9 2.1 %copy.11 = bf16[1536,256]{1,0:T(8,128)(2,1)} copy(bf16[1536,256]{1,0:T(8,128)(2,1)} %shard_map.64) | data formatting | bytes 1572864

commit v2 on v1

--- a/solution.py
+++ b/solution.py
@@ -17,8 +17,8 @@
 
 
 def kernel(
-    tokens, weight, taps, residues, decay, skip, out,
-    tok, w, proj, query, base, states, mixed, carry, lam, filt, scan, bdec, gdec, lead, tapb, skipb,
+    tokens, weight, taps_in, residues_in, decay_in, skip_in, out,
+    taps, residues, decay, skip, tok, w, proj, query, base, states, mixed, carry, lam, filt, scan, bdec, gdec, lead, tapb, skipb,
     final, landed, entry,
     s_send, s_recv, w_send_sem, w_recv_sem, h_send, h_recv, f_send, f_recv, local,
 ):
@@ -26,7 +26,7 @@
     x, y, z, core = ch // 4, ch % 4, ctx // 2, ctx % 2
     sibling = z * 2 + 1 - core
     rows = tokens.shape[0]
-    poles = residues.shape[0]
+    poles = residues_in.shape[0]
     groups = rows // GROUP
     nctx = 16
 
@@ -34,16 +34,24 @@
         return {"ch": (x + d) % 4 * 4 + y if axis == "x" else x * 4 + (y + d) % 4}
 
     own_tok = pltpu.make_async_copy(tokens, tok.at[x, y], local.at[0])
-    own_w = pltpu.make_async_copy(weight, w.at[pl.ds(ctx * 256, 256)], local.at[1])
+    own_w = pltpu.make_async_copy(weight, w.at[:, pl.ds(ctx * 256, 256)], local.at[1])
     own_tok.start()
     own_w.start()
+    small = [
+        pltpu.make_async_copy(src, dst, local.at[2 + i])
+        for i, (src, dst) in enumerate(
+            ((taps_in, taps), (residues_in, residues), (decay_in, decay), (skip_in, skip))
+        )
+    ]
+    for copy in small:
+        copy.start()
     barrier = pltpu.get_barrier_semaphore()
     for axis in "xy":
         for d in (1, 3):
             pl.semaphore_signal(barrier, 1, device_id=near(axis, d), device_id_type=MESH)
-    for o in range(1, nctx):
+    for o in (1, 2, nctx - 2, nctx - 1):
         pl.semaphore_signal(barrier, 1, device_id={"ctx": (ctx + o) % nctx}, device_id_type=MESH)
-    pl.semaphore_wait(barrier, 4 + nctx - 1)
+    pl.semaphore_wait(barrier, 8)
     own_tok.wait()
     own_w.wait()
 
@@ -97,7 +105,7 @@
                     if s == 4 and part != i:
                         continue
                     copies["w", s - 1, i, part].wait_recv()
-                ref = w.at[pl.ds(owner * 256 + part * 128, 128)]
+                ref = w.at[:, pl.ds(owner * 256 + part * 128, 128)]
                 if s < 3 or (s == 3 and part == i):
                     to = {"ctx": (z + d) % 8 * 2 + core}
                     send(("w", s, i, part), ref, to, w_send_sem.at[s, i, part], w_recv_sem.at[s, i, part])
@@ -107,47 +115,46 @@
                         w_send_sem.at[s, 2 + i, part], w_recv_sem.at[s, 2 + i, part],
                     )
 
-    def tables():
+    def tables(t):
         ids = lax.broadcasted_iota(jnp.int32, (8, 128), 0)
         lanes8 = ids.astype(F32)
-        for t in (0, 1):
-            cols = pl.ds(t * 128, 128)
-            for g in range(3):
-                for k in range(3):
-                    tapb[t, g * 3 + k] = jnp.broadcast_to(taps[g, k : k + 1, cols], (8, 128))
-            skipb[t] = jnp.broadcast_to(skip[:, cols], (8, 128))
+        cols = pl.ds(t * 128, 128)
+        for g in range(3):
+            for k in range(3):
+                tapb[t, g * 3 + k] = jnp.broadcast_to(taps[g, k : k + 1, cols], (8, 128))
+        skipb[t] = jnp.broadcast_to(skip[:, cols], (8, 128))
+        for m in range(L):
+            filt[t, m] = jnp.zeros((8, 128), F32)
+        for n in range(poles):
+            lam[t, n] = jnp.broadcast_to(decay[n : n + 1, cols], (8, 128))
+            lead[t, n] = jnp.broadcast_to(residues[n : n + 1, cols], (8, 128))
+
+        def mode(n, _):
+            rate, gain = lam[t, n], lead[t, n]
+            step = jnp.exp(-rate)
+            lam[t, n] = step
+            lead[t, n] = gain * step
+            for k, s in enumerate((1, 2, 4)):
+                scan[t, k, n] = jnp.where(ids >= s, jnp.exp(-rate * float(L * s)), 0.0)
+            bdec[t, n] = jnp.exp(-rate * (lanes8 * float(L)))
+            gdec[t, n] = jnp.exp(-rate * float(GROUP))
+            carry[t, n] = jnp.zeros((8, 128), F32)
             for m in range(L):
-                filt[t, m] = jnp.zeros((8, 128), F32)
-            for n in range(poles):
-                lam[t, n] = jnp.broadcast_to(decay[n : n + 1, cols], (8, 128))
-                lead[t, n] = jnp.broadcast_to(residues[n : n + 1, cols], (8, 128))
-
-            def mode(n, _):
-                rate, gain = lam[t, n], lead[t, n]
-                step = jnp.exp(-rate)
-                lam[t, n] = step
-                lead[t, n] = gain * step
-                for k, s in enumerate((1, 2, 4)):
-                    scan[t, k, n] = jnp.where(ids >= s, jnp.exp(-rate * float(L * s)), 0.0)
-                bdec[t, n] = jnp.exp(-rate * (lanes8 * float(L)))
-                gdec[t, n] = jnp.exp(-rate * float(GROUP))
-                carry[t, n] = jnp.zeros((8, 128), F32)
-                for m in range(L):
-                    filt[t, m] += gain * jnp.exp(-rate * float(m))
-                return 0
-
-            lax.fori_loop(0, poles, mode, 0)
+                filt[t, m] += gain * jnp.exp(-rate * float(m))
+            return 0
+
+        lax.fori_loop(0, poles, mode, 0)
 
     def project(first, size):
         span = pl.ds(first, size)
         left = jnp.concatenate([tok[i // 4, i % 4, span, :] for i in range(16)], axis=1)
         for g in range(3):
-            total = jnp.dot(left, w[:, g * 256 : (g + 1) * 256], preferred_element_type=F32)
+            total = jnp.dot(left, w[g], preferred_element_type=F32)
             total = total.astype(BF16).astype(F32)
             for t in (0, 1):
                 proj[g * 2 + t, pl.ds(HALO + first, size), :] = total[:, t * 128 : (t + 1) * 128]
 
-    def filter_group(g, t):
+    def filter_group(g, t, convolve):
         first = HALO + g * GROUP
         ids = lax.broadcasted_iota(jnp.int32, (8, 128), 0)
 
@@ -182,43 +189,56 @@
             states[g, t, n] = before + bdec[t, n] * held
             carry[t, n] = jnp.broadcast_to(end[7:8], (8, 128)) + gdec[t, n] * held
 
+        if convolve:
+            convolve_group(g, t, gated)
+        else:
+            for i in range(L):
+                base[g, t, i] = gated[i]
+
+    def convolve_group(g, t, gated):
         for i in range(L):
             total = skipb[t] * gated[i]
             for j in range(i + 1):
                 total = total + filt[t, i - j] * gated[j]
             base[g, t, i] = total
 
-    def filter_groups(lo, hi):
+    def filter_groups(lo, hi, convolve=True):
         def step(k, _):
-            filter_group(lo + k // 2, k % 2)
+            filter_group(lo + k // 2, k % 2, convolve)
             return 0
 
         lax.fori_loop(0, 2 * (hi - lo), step, 0)
 
-    def finish(k, _):
-        g, t = k // 2, k % 2
-        flow = []
-        for n in range(poles):
-            held = entry[t, n]
-            flow.append(lead[t, n] * (states[g, t, n] + bdec[t, n] * held))
-            entry[t, n] = gdec[t, n] * held
-        steps = [lam[t, n] for n in range(poles)]
-        for i in range(L):
-            parts = flow
-            while len(parts) > 1:
-                parts = [a + b for a, b in zip(parts[::2], parts[1::2])]
-            mixed[t, pl.ds(g * GROUP + i, 8, stride=L), :] = query[g, t, i] * (base[g, t, i] + parts[0])
-            if i < L - 1:
-                flow = [a * b for a, b in zip(flow, steps)]
+    def convolve_groups(lo, hi):
+        def step(k, _):
+            g, t = lo + k // 2, k % 2
+            convolve_group(g, t, [base[g, t, i] for i in range(L)])
+            return 0
+
+        lax.fori_loop(0, 2 * (hi - lo), step, 0)
+
+    def finish(g, _):
         span = pl.ds(pl.multiple_of(g * GROUP, GROUP), GROUP)
-        out[span, pl.ds(pl.multiple_of(t * 128, 128), 128)] = mixed[t, span, :].astype(BF16)
+        for t in (0, 1):
+            flow = []
+            for n in range(poles):
+                held = entry[t, n]
+                flow.append(lead[t, n] * (states[g, t, n] + bdec[t, n] * held))
+                entry[t, n] = gdec[t, n] * held
+            for i in range(L):
+                parts = flow
+                while len(parts) > 1:
+                    parts = [a + b for a, b in zip(parts[::2], parts[1::2])]
+                mixed[t, pl.ds(g * GROUP + i, 8, stride=L), :] = query[g, t, i] * (base[g, t, i] + parts[0])
+                if i < L - 1:
+                    flow = [a * lam[t, n] for n, a in enumerate(flow)]
+            out[span, t * 128 : (t + 1) * 128] = mixed[t, span, :].astype(BF16)
         return 0
 
     count = len(CHUNKS)
     weights(0)
     for r in range(count):
         stage(r, 1, 0)
-    tables()
     for r in range(count):
         stage(r, 1, 1)
     weights(1)
@@ -236,14 +256,13 @@
 
     def compute(r):
         landed_stage(r, 2)
-        first, size = CHUNKS[r]
-        if size == 128:
-            project(first, size)
-        else:
-            for half in range(0, size, 256):
-                project(first + half, 256)
-
+        project(*CHUNKS[r])
+
+    for copy in small:
+        copy.wait()
+    tables(0)
     tick(0)
+    tables(1)
     weights(2)
     tick(1)
     weights(3)
@@ -267,16 +286,15 @@
     def _():
         halo.start()
 
+    tick(3)
     compute(1)
+    compute(2)
 
     @pl.when(ctx > 0)
     def _():
         halo.wait_recv()
 
-    filter_groups(0, 2)
-    tick(3)
-    compute(2)
-    filter_groups(2, 4)
+    filter_groups(0, 4)
     tick(4)
     compute(3)
     filter_groups(4, 6)
@@ -287,11 +305,11 @@
     compute(5)
     filter_groups(8, 10)
     compute(6)
-    filter_groups(10, 12)
+    filter_groups(10, 12, False)
 
     for t in (0, 1):
-        for n in range(poles):
-            final[n : n + 1, t * 128 : (t + 1) * 128] = carry[t, n, 0:1, :]
+        held = jnp.concatenate([carry[t, n, 0:1, :] for n in range(poles)], axis=0)
+        final[:, t * 128 : (t + 1) * 128] = held.astype(BF16)
 
     def exchange(o):
         return pltpu.make_async_remote_copy(
@@ -306,6 +324,7 @@
         def _():
             exchange(o).start()
 
+    convolve_groups(10, 12)
     for o in range(1, nctx):
 
         @pl.when(ctx >= o)
@@ -319,13 +338,13 @@
     across = jnp.exp(-decay[...] * float(rows))
 
     def join(k, total):
-        return across * total + landed[k]
+        return across * total + landed[k].astype(F32)
 
     incoming = lax.fori_loop(0, ctx, join, jnp.zeros((poles, 256), F32))
     for t in (0, 1):
         for n in range(poles):
             entry[t, n] = jnp.broadcast_to(incoming[n : n + 1, t * 128 : (t + 1) * 128], (8, 128))
-    lax.fori_loop(0, 2 * groups, finish, 0)
+    lax.fori_loop(0, groups, finish, 0)
 
     for copy in sent:
         copy.wait_send()
@@ -346,15 +365,19 @@
     groups = rows // GROUP
     flops = 2 * rows * 4096 * 768
     dma = pltpu.SemaphoreType.DMA
-    vmem, anywhere = pl.BlockSpec(memory_space=pltpu.VMEM), pl.BlockSpec(memory_space=pl.ANY)
+    anywhere = pl.BlockSpec(memory_space=pl.ANY)
     return pl.pallas_call(
         kernel,
-        out_shape=jax.ShapeDtypeStruct((rows, 256), BF16),
-        in_specs=[anywhere, anywhere, vmem, vmem, vmem, vmem],
-        out_specs=vmem,
+        out_shape=pltpu.VMEM((rows, 256), BF16),
+        in_specs=[anywhere] * 6,
+        out_specs=pl.BlockSpec(memory_space=pltpu.VMEM),
         scratch_shapes=[
+            pltpu.VMEM((3, 3, 256), F32),
+            pltpu.VMEM((poles, 256), F32),
+            pltpu.VMEM((poles, 256), F32),
+            pltpu.VMEM((1, 256), F32),
             pltpu.VMEM((4, 4, rows, 256), BF16),
-            pltpu.VMEM((4096, 768), BF16),
+            pltpu.VMEM((3, 4096, 256), BF16),
             pltpu.VMEM((6, HALO + rows, 128), F32),
             pltpu.VMEM((groups, 2, L, 8, 128), F32),
             pltpu.VMEM((groups, 2, L, 8, 128), F32),
@@ -369,8 +392,8 @@
             pltpu.VMEM((2, poles, 8, 128), F32),
             pltpu.VMEM((2, 9, 8, 128), F32),
             pltpu.VMEM((2, 8, 128), F32),
-            pltpu.VMEM((poles, 256), F32),
-            pltpu.VMEM((16, poles, 256), F32),
+            pltpu.VMEM((poles, 256), BF16),
+            pltpu.VMEM((16, poles, 256), BF16),
             pltpu.VMEM((2, poles, 8, 128), F32),
             dma((len(CHUNKS), 16)),
             dma((len(CHUNKS), 16)),
@@ -380,13 +403,13 @@
             dma(()),
             dma((16,)),
             dma((16,)),
-            dma((2,)),
+            dma((6,)),
         ],
         compiler_params=pltpu.CompilerParams(
             collective_id=0, has_side_effects=True, vmem_limit_bytes=56 * 2**20
         ),
         cost_estimate=pl.CostEstimate(flops=flops, bytes_accessed=4 * 2**20, transcendentals=0),
-    )(tokens, in_weight.reshape(256, 768), short_taps, residues, decay_rates, skip_gain.reshape(1, 256))
+    )(tokens, in_weight.transpose(1, 0, 2), short_taps, residues, decay_rates, skip_gain.reshape(1, 256))
 
 
 def solution(mesh):

time: 95.1 us -> 85.8 us (0.902)
  the two profiles are of different devices: /device:TPU:199 before, /device:TPU:1 now
where the time goes in v2:
time: 85.8 us; the launch traced here: 85.6 us
  Pallas kernels  84.7 us (99%)
  local copies, waits for them, and re-layouts  0.88 us (1%)
    pallas_call x1, Pallas kernels, body(): pl.pallas_call(kernel, out_shape=pltpu.VMEM((rows, 256), BF16), in_specs=...  84.7 us

profile of v2, /device:TPU:1, one launch (start us, length us, event | category | flops | bytes accessed | tf_op | source)
XLA Modules:
  0.0 85.6 jit_solution(11909453947763871098)
XLA Ops:
  0.0 84.7 %shard_map.64 = bf16[1536,256]{1,0:T(8,128)(2,1)S(1)} custom-call(bf16[1536,256]{1,0:T(8,128)(2,1)} %tokens.1, bf16[3,256,256]{2,1,0:T(8,128)(2,1)} %bitcast.2, f32[3,3,256]{2,1,0:T(4,128)} %taps_in.1, f32[16,256]{1,0:T(8,128)} %residues_in.1, f32[16,256]{1,0:T(8,128)} %decay_in.1, f32[1,256]{1,0:T(1,128)} %bitcast.3), custom_call_target="tpu_custom_call" | custom-call | flops 9663676416 | bytes 4194304 | tf_op jit(solution)/shard_map/pallas_call | solution.py:369
  84.8 0.9 %copy.8 = bf16[1536,256]{1,0:T(8,128)(2,1)} copy(bf16[1536,256]{1,0:T(8,128)(2,1)S(1)} %shard_map.64) | data formatting | bytes 1572864

commit v3 on v2

--- a/solution.py
+++ b/solution.py
@@ -13,13 +13,14 @@
 L = 16
 GROUP = 8 * L
 HALO = 8
-CHUNKS = ((1408, 128), (0, 256), (256, 256), (512, 256), (768, 256), (1024, 256), (1280, 128))
+LATE = 1024
+CHUNKS = ((1408, 128), (0, 384), (384, 384), (768, 256), (1024, 256), (1280, 128))
 
 
 def kernel(
     tokens, weight, taps_in, residues_in, decay_in, skip_in, out,
     taps, residues, decay, skip, tok, w, proj, query, base, states, mixed, carry, lam, filt, scan, bdec, gdec, lead, tapb, skipb,
-    final, landed, entry,
+    final, landed, entry, partial,
     s_send, s_recv, w_send_sem, w_recv_sem, h_send, h_recv, f_send, f_recv, local,
 ):
     ch, ctx = lax.axis_index("ch"), lax.axis_index("ctx")
@@ -33,6 +34,12 @@
     def near(axis, d):
         return {"ch": (x + d) % 4 * 4 + y if axis == "x" else x * 4 + (y + d) % 4}
 
+    barrier = pltpu.get_barrier_semaphore()
+    for axis in "xy":
+        for d in (1, 3):
+            pl.semaphore_signal(barrier, 1, device_id=near(axis, d), device_id_type=MESH)
+    for o in (1, 2, nctx - 2, nctx - 1):
+        pl.semaphore_signal(barrier, 1, device_id={"ctx": (ctx + o) % nctx}, device_id_type=MESH)
     own_tok = pltpu.make_async_copy(tokens, tok.at[x, y], local.at[0])
     own_w = pltpu.make_async_copy(weight, w.at[:, pl.ds(ctx * 256, 256)], local.at[1])
     own_tok.start()
@@ -45,12 +52,6 @@
     ]
     for copy in small:
         copy.start()
-    barrier = pltpu.get_barrier_semaphore()
-    for axis in "xy":
-        for d in (1, 3):
-            pl.semaphore_signal(barrier, 1, device_id=near(axis, d), device_id_type=MESH)
-    for o in (1, 2, nctx - 2, nctx - 1):
-        pl.semaphore_signal(barrier, 1, device_id={"ctx": (ctx + o) % nctx}, device_id_type=MESH)
     pl.semaphore_wait(barrier, 8)
     own_tok.wait()
     own_w.wait()
@@ -145,50 +146,65 @@
 
         lax.fori_loop(0, poles, mode, 0)
 
-    def project(first, size):
+    def project(first, size, parts):
         span = pl.ds(first, size)
         left = jnp.concatenate([tok[i // 4, i % 4, span, :] for i in range(16)], axis=1)
-        for g in range(3):
+        for g in parts:
             total = jnp.dot(left, w[g], preferred_element_type=F32)
-            total = total.astype(BF16).astype(F32)
-            for t in (0, 1):
-                proj[g * 2 + t, pl.ds(HALO + first, size), :] = total[:, t * 128 : (t + 1) * 128]
+            keep(first, size, g, total)
+
+    def keep(first, size, part, total):
+        total = total.astype(BF16).astype(F32)
+        for t in (0, 1):
+            proj[part * 2 + t, pl.ds(HALO + first, size), :] = total[:, t * 128 : (t + 1) * 128]
+
+    def product(first, size, h, part, steps):
+        total = None
+        for k in steps:
+            for i in range(4):
+                at_x, at_y = (i, (y + k) % 4) if h == 0 else ((x + k) % 4, i)
+                rows_of = pl.ds(pl.multiple_of((at_x * 4 + at_y) * 256, 256), 256)
+                one = jnp.dot(
+                    tok[at_x, at_y, pl.ds(first, size), :], w[part, rows_of, :], preferred_element_type=F32
+                )
+                total = one if total is None else total + one
+        return total
+
+    def begin(r):
+        for _, _, first, size, h in halves(r):
+            for part in range(3):
+                partial[part, pl.ds(first - LATE, size), :] = product(first, size, h, part, (0, 1, 3))
+
+    def complete(r, parts):
+        for _, _, first, size, h in halves(r):
+            for part in parts:
+                total = partial[part, pl.ds(first - LATE, size), :] + product(first, size, h, part, (2,))
+                keep(first, size, part, total)
+
+    def features(g, t, part):
+        first = HALO + g * GROUP
+        k0, k1, k2 = (tapb[t, part * 3 + k] for k in range(3))
+        rows_at = [proj[part * 2 + t, pl.ds(first + i, 8, stride=L), :] for i in range(-2, L)]
+        return [k0 * rows_at[i + 2] + k1 * rows_at[i + 1] + k2 * rows_at[i] for i in range(L)]
 
     def filter_group(g, t, convolve):
-        first = HALO + g * GROUP
         ids = lax.broadcasted_iota(jnp.int32, (8, 128), 0)
-
-        def rows_at(part, i):
-            return proj[part * 2 + t, pl.ds(first + i, 8, stride=L), :]
-
-        feats = []
-        for part in range(3):
-            k0, k1, k2 = (tapb[t, part * 3 + k] for k in range(3))
-            two, one = rows_at(part, -2), rows_at(part, -1)
-            listed = []
-            for i in range(L):
-                now = rows_at(part, i)
-                value = k0 * now + k1 * one + k2 * two
-                if part == 0:
-                    query[g, t, i] = value
-                else:
-                    listed.append(value)
-                two, one = one, now
-            feats.append(listed)
-        gated = [(a * b).astype(BF16).astype(F32) for a, b in zip(feats[1], feats[2])]
-
-        for n in range(poles):
-            step = lam[t, n]
-            end = gated[0]
+        gated = [(a * b).astype(BF16).astype(F32) for a, b in zip(features(g, t, 1), features(g, t, 2))]
+
+        for lo in range(0, poles, 8):
+            modes = range(lo, lo + 8)
+            steps = [lam[t, n] for n in modes]
+            held = [carry[t, n] for n in modes]
+            ends = [gated[0]] * 8
             for i in range(1, L):
-                end = step * end + gated[i]
+                ends = [a * b + gated[i] for a, b in zip(steps, ends)]
             for k, s in enumerate((1, 2, 4)):
-                end = end + scan[t, k, n] * pltpu.roll(end, s, axis=0)
-            before = jnp.where(ids >= 1, pltpu.roll(end, 1, axis=0), 0.0)
-            held = carry[t, n]
-            states[g, t, n] = before + bdec[t, n] * held
-            carry[t, n] = jnp.broadcast_to(end[7:8], (8, 128)) + gdec[t, n] * held
-
+                ends = [e + scan[t, k, n] * pltpu.roll(e, s, axis=0) for n, e in zip(modes, ends)]
+            before = [jnp.where(ids >= 1, pltpu.roll(e, 1, axis=0), 0.0) for e in ends]
+            for n, a, b in zip(modes, before, held):
+                states[g, t, n] = a + bdec[t, n] * b
+            for n, e, b in zip(modes, ends, held):
+                carry[t, n] = jnp.broadcast_to(e[7:8], (8, 128)) + gdec[t, n] * b
         if convolve:
             convolve_group(g, t, gated)
         else:
@@ -196,11 +212,15 @@
                 base[g, t, i] = gated[i]
 
     def convolve_group(g, t, gated):
+        for i, value in enumerate(features(g, t, 0)):
+            query[g, t, i] = value
+        taken = [filt[t, m] for m in range(L)]
+        totals = [skipb[t] * a for a in gated]
+        for j in range(L):
+            for i in range(j, L):
+                totals[i] = totals[i] + taken[i - j] * gated[j]
         for i in range(L):
-            total = skipb[t] * gated[i]
-            for j in range(i + 1):
-                total = total + filt[t, i - j] * gated[j]
-            base[g, t, i] = total
+            base[g, t, i] = totals[i]
 
     def filter_groups(lo, hi, convolve=True):
         def step(k, _):
@@ -220,7 +240,7 @@
     def finish(g, _):
         span = pl.ds(pl.multiple_of(g * GROUP, GROUP), GROUP)
         for t in (0, 1):
-            flow = []
+            flow, steps = [], [lam[t, n] for n in range(poles)]
             for n in range(poles):
                 held = entry[t, n]
                 flow.append(lead[t, n] * (states[g, t, n] + bdec[t, n] * held))
@@ -231,13 +251,14 @@
                     parts = [a + b for a, b in zip(parts[::2], parts[1::2])]
                 mixed[t, pl.ds(g * GROUP + i, 8, stride=L), :] = query[g, t, i] * (base[g, t, i] + parts[0])
                 if i < L - 1:
-                    flow = [a * lam[t, n] for n, a in enumerate(flow)]
+                    flow = [a * b for a, b in zip(flow, steps)]
             out[span, t * 128 : (t + 1) * 128] = mixed[t, span, :].astype(BF16)
         return 0
 
     count = len(CHUNKS)
+    stage(0, 1, 0)
     weights(0)
-    for r in range(count):
+    for r in range(1, count):
         stage(r, 1, 0)
     for r in range(count):
         stage(r, 1, 1)
@@ -254,9 +275,9 @@
         if r + 2 < count:
             stage(r + 2, 2, 0)
 
-    def compute(r):
+    def compute(r, parts=(0, 1, 2)):
         landed_stage(r, 2)
-        project(*CHUNKS[r])
+        project(*CHUNKS[r], parts)
 
     for copy in small:
         copy.wait()
@@ -286,56 +307,56 @@
     def _():
         halo.start()
 
+    compute(1)
     tick(3)
-    compute(1)
-    compute(2)
 
     @pl.when(ctx > 0)
     def _():
         halo.wait_recv()
 
-    filter_groups(0, 4)
+    filter_groups(0, 3)
+    compute(2)
+    filter_groups(3, 6)
+    early = len(sent)
     tick(4)
     compute(3)
-    filter_groups(4, 6)
+    filter_groups(6, 8)
     tick(5)
-    compute(4)
-    filter_groups(6, 8)
-    tick(6)
-    compute(5)
+    begin(4)
+    for copy in sent[:early]:
+        copy.wait_send()
+    landed_stage(4, 2)
+    complete(4, (0, 1, 2))
     filter_groups(8, 10)
-    compute(6)
+    compute(5, (1, 2))
     filter_groups(10, 12, False)
 
     for t in (0, 1):
-        held = jnp.concatenate([carry[t, n, 0:1, :] for n in range(poles)], axis=0)
-        final[:, t * 128 : (t + 1) * 128] = held.astype(BF16)
-
-    def exchange(o):
+        final[:, t * 128 : (t + 1) * 128] = jnp.concatenate([carry[t, n, 0:1, :] for n in range(poles)], axis=0).astype(BF16)
+
+    def exchange(o, slot):
         return pltpu.make_async_remote_copy(
-            src_ref=final, dst_ref=landed.at[ctx],
+            src_ref=final, dst_ref=landed.at[slot],
             send_sem=f_send.at[o], recv_sem=f_recv.at[o],
             device_id={"ctx": (ctx + o) % nctx}, device_id_type=MESH,
         )
 
-    for o in range(1, nctx):
+    for o in range(nctx - 1, 0, -1):
 
         @pl.when(ctx + o < nctx)
         def _():
-            exchange(o).start()
-
+            exchange(o, ctx).start()
+
+    project(*CHUNKS[5], (0,))
     convolve_groups(10, 12)
+    for copy in sent[early:]:
+        copy.wait_send()
+    across = jnp.exp(-decay[...] * float(rows))
     for o in range(1, nctx):
 
         @pl.when(ctx >= o)
         def _():
-            pltpu.make_async_remote_copy(
-                src_ref=final, dst_ref=landed.at[(ctx - o) % nctx],
-                send_sem=f_send.at[o], recv_sem=f_recv.at[o],
-                device_id={"ctx": (ctx + o) % nctx}, device_id_type=MESH,
-            ).wait_recv()
-
-    across = jnp.exp(-decay[...] * float(rows))
+            exchange(o, (ctx - o) % nctx).wait_recv()
 
     def join(k, total):
         return across * total + landed[k].astype(F32)
@@ -346,8 +367,6 @@
             entry[t, n] = jnp.broadcast_to(incoming[n : n + 1, t * 128 : (t + 1) * 128], (8, 128))
     lax.fori_loop(0, groups, finish, 0)
 
-    for copy in sent:
-        copy.wait_send()
 
     @pl.when(ctx < nctx - 1)
     def _():
@@ -357,7 +376,7 @@
 
         @pl.when(ctx + o < nctx)
         def _():
-            exchange(o).wait_send()
+            exchange(o, ctx).wait_send()
 
 
 def body(tokens, in_weight, short_taps, residues, decay_rates, skip_gain):
@@ -395,6 +414,7 @@
             pltpu.VMEM((poles, 256), BF16),
             pltpu.VMEM((16, poles, 256), BF16),
             pltpu.VMEM((2, poles, 8, 128), F32),
+            pltpu.VMEM((3, 256, 256), F32),
             dma((len(CHUNKS), 16)),
             dma((len(CHUNKS), 16)),
             dma((5, 4, 2)),

time: 85.8 us -> 84.8 us (0.988)
  Pallas kernels: 84.7 us -> 83.7 us
    pallas_call x1, Pallas kernels: 84.7 us -> 83.7 us  [body(): pl.pallas_call(kernel, out_shape=pltpu.VMEM((rows, 256), BF16), in_specs=...]
where the time goes in v3:
time: 84.8 us; the launch traced here: 84.6 us
  Pallas kernels  83.7 us (99%)
  local copies, waits for them, and re-layouts  0.88 us (1%)
    pallas_call x1, Pallas kernels, body(): pl.pallas_call(kernel, out_shape=pltpu.VMEM((rows, 256), BF16), in_specs=...  83.7 us

profile of v3, /device:TPU:1, one launch (start us, length us, event | category | flops | bytes accessed | tf_op | source)
XLA Modules:
  0.0 84.6 jit_solution(11483176092780391809)
XLA Ops:
  0.0 83.7 %shard_map.64 = bf16[1536,256]{1,0:T(8,128)(2,1)S(1)} custom-call(bf16[1536,256]{1,0:T(8,128)(2,1)} %tokens.1, bf16[3,256,256]{2,1,0:T(8,128)(2,1)} %bitcast.2, f32[3,3,256]{2,1,0:T(4,128)} %taps_in.1, f32[16,256]{1,0:T(8,128)} %residues_in.1, f32[16,256]{1,0:T(8,128)} %decay_in.1, f32[1,256]{1,0:T(1,128)} %bitcast.3), custom_call_target="tpu_custom_call" | custom-call | flops 9663676416 | bytes 4194304 | tf_op jit(solution)/shard_map/pallas_call | solution.py:388
  83.7 0.9 %copy.8 = bf16[1536,256]{1,0:T(8,128)(2,1)} copy(bf16[1536,256]{1,0:T(8,128)(2,1)S(1)} %shard_map.64) | data formatting | bytes 1572864

commit v4 on v3

--- a/solution.py
+++ b/solution.py
@@ -14,7 +14,7 @@
 GROUP = 8 * L
 HALO = 8
 LATE = 1024
-CHUNKS = ((1408, 128), (0, 384), (384, 384), (768, 256), (1024, 256), (1280, 128))
+CHUNKS = ((1408, 128), (0, 640), (640, 384), (1024, 256), (1280, 128))
 
 
 def kernel(
@@ -314,21 +314,18 @@
     def _():
         halo.wait_recv()
 
-    filter_groups(0, 3)
+    filter_groups(0, 5)
+    early = len(sent)
     compute(2)
-    filter_groups(3, 6)
-    early = len(sent)
     tick(4)
-    compute(3)
-    filter_groups(6, 8)
-    tick(5)
-    begin(4)
+    filter_groups(5, 8)
+    begin(3)
     for copy in sent[:early]:
         copy.wait_send()
-    landed_stage(4, 2)
-    complete(4, (0, 1, 2))
-    filter_groups(8, 10)
-    compute(5, (1, 2))
+    landed_stage(3, 2)
+    complete(3, (0, 1, 2))
+    filter_groups(8, 10, False)
+    compute(4, (1, 2))
     filter_groups(10, 12, False)
 
     for t in (0, 1):
@@ -341,14 +338,14 @@
             device_id={"ctx": (ctx + o) % nctx}, device_id_type=MESH,
         )
 
-    for o in range(nctx - 1, 0, -1):
+    for o in range(1, nctx):
 
         @pl.when(ctx + o < nctx)
         def _():
             exchange(o, ctx).start()
 
-    project(*CHUNKS[5], (0,))
-    convolve_groups(10, 12)
+    project(*CHUNKS[4], (0,))
+    convolve_groups(8, 12)
     for copy in sent[early:]:
         copy.wait_send()
     across = jnp.exp(-decay[...] * float(rows))
@@ -397,11 +394,11 @@
             pltpu.VMEM((1, 256), F32),
             pltpu.VMEM((4, 4, rows, 256), BF16),
             pltpu.VMEM((3, 4096, 256), BF16),
-            pltpu.VMEM((6, HALO + rows, 128), F32),
+            pltpu.VMEM((6, HALO + rows + L, 128), F32),
             pltpu.VMEM((groups, 2, L, 8, 128), F32),
             pltpu.VMEM((groups, 2, L, 8, 128), F32),
             pltpu.VMEM((groups, 2, poles, 8, 128), F32),
-            pltpu.VMEM((2, rows, 128), F32),
+            pltpu.VMEM((2, rows + L, 128), F32),
             pltpu.VMEM((2, poles, 8, 128), F32),
             pltpu.VMEM((2, poles, 8, 128), F32),
             pltpu.VMEM((2, L, 8, 128), F32),

time: 84.8 us -> 84.5 us (level)
  no operation moved by 1% of the time
where the time goes in v4:
time: 84.5 us; the launch traced here: 84.4 us
  Pallas kernels  83.5 us (99%)
  local copies, waits for them, and re-layouts  0.88 us (1%)
    pallas_call x1, Pallas kernels, body(): pl.pallas_call(kernel, out_shape=pltpu.VMEM((rows, 256), BF16), in_specs=...  83.5 us

profile of v4, /device:TPU:1, one launch (start us, length us, event | category | flops | bytes accessed | tf_op | source)
XLA Modules:
  0.0 84.4 jit_solution(12937194363040023369)
XLA Ops:
  0.0 83.5 %shard_map.64 = bf16[1536,256]{1,0:T(8,128)(2,1)S(1)} custom-call(bf16[1536,256]{1,0:T(8,128)(2,1)} %tokens.1, bf16[3,256,256]{2,1,0:T(8,128)(2,1)} %bitcast.2, f32[3,3,256]{2,1,0:T(4,128)} %taps_in.1, f32[16,256]{1,0:T(8,128)} %residues_in.1, f32[16,256]{1,0:T(8,128)} %decay_in.1, f32[1,256]{1,0:T(1,128)} %bitcast.3), custom_call_target="tpu_custom_call" | custom-call | flops 9663676416 | bytes 4194304 | tf_op jit(solution)/shard_map/pallas_call | solution.py:385
  83.5 0.9 %copy.8 = bf16[1536,256]{1,0:T(8,128)(2,1)} copy(bf16[1536,256]{1,0:T(8,128)(2,1)S(1)} %shard_map.64) | data formatting | bytes 1572864
